TPU v7x, 32 devices: a whole 2x2x4 slice. The times are simulated.
32 devices in a mesh: groups: 2 (over y), seq: 16 (over z, x, core).
Axes of the slice: x: 2, y: 2, z: 4, core: 2. Of those that a mesh axis runs over, the one named last changes fastest.
Arguments:
- qkv: bfloat16 [4096, 32, 384], P(('groups', 'seq')), parts along dimension 0
- routes: int32 [4096, 32], P(('groups', 'seq')), parts along dimension 0, may hold values from 0 to 1, as said below
Outputs:
- attended: bfloat16 [4096, 32, 128], P(('groups', 'seq')), parts along dimension 0
There are 2 independent parts, one for each index of `groups`. A program takes and returns all parts, laid end to end along the dimension named above; each array names one. Nothing has to cross between parts.
Inputs may be any that keep to these rules, and one draw needn't show every extreme that they name: Every cluster of every head holds between 512 and 1536 tokens, and in every head some cluster holds exactly 1536. Numbering the pairs (head h, cluster c) as h * 2 + c, the tokens of one device name each aligned group of 4 pairs exactly 256 times. Integer counts, offsets and slot indices derived from routes may cross between devices packed several to a 32-bit word.
All inputs are finite; a program needn't handle non-finite values.
Results may differ from a plain program's by a relative error of at most 0.0047.
Values may be sent and summed in bfloat16 or wider, within the bound.
A program may use at most 128 MiB of HBM per device.

v0:
```python
import math

import jax
import jax.numpy as jnp
from jax import lax
from jax.sharding import PartitionSpec as P

CLEN = 1024


def entering(part, axis, combine, identity):
    place = lax.axis_index(axis)
    gathered = lax.all_gather(part, axis)
    state = jnp.zeros_like(part) + jnp.asarray(identity, part.dtype)

    def one(turn, state):
        return combine(state, lax.dynamic_index_in_dim(gathered, turn, 0, False))

    return lax.fori_loop(0, place, one, state)


def attend(queries, keys, values, start, scale):
    block_rows = queries.shape[1]
    span = keys.shape[1]
    scores = jnp.einsum("pqd,pkd->pqk", queries, keys, preferred_element_type=jnp.float32) * scale
    rows = start + jnp.arange(block_rows, dtype=jnp.int32)[:, None]
    cols = jnp.arange(span, dtype=jnp.int32)[None, :]
    scores = jnp.where((cols <= rows)[None], scores, -1e30)
    peak = jnp.max(scores, axis=2, keepdims=True)
    expo = jnp.exp(scores - peak)
    weights = (expo / jnp.sum(expo, axis=2, keepdims=True)).astype(jnp.bfloat16)
    return jnp.einsum("pqk,pkd->pqd", weights, values, preferred_element_type=jnp.float32).astype(
        jnp.bfloat16
    )


def local(qkv, routes):
    tok, heads, width = qkv.shape
    head_size = width // 3
    nseq = lax.axis_size("seq")
    clusters = nseq * tok // CLEN
    pairs_dev = heads * tok // CLEN
    capacity = 3 * CLEN // 2
    block_rows = CLEN // 2
    share = CLEN // nseq
    rows_peer = pairs_dev * share
    total_pairs = heads * clusters
    scale = 1.0 / math.sqrt(head_size)
    member = routes[:, :, None] == jnp.arange(clusters, dtype=jnp.int32)[None, None, :]
    member_flat = member.reshape(tok, total_pairs)
    counts = jnp.sum(member_flat.astype(jnp.int32), axis=0)
    earlier = (jnp.arange(tok)[:, None] > jnp.arange(tok)[None, :]).astype(jnp.bfloat16)
    before = jnp.dot(earlier, member_flat.astype(jnp.bfloat16), preferred_element_type=jnp.float32)
    rank = jnp.sum(jnp.where(member, before.reshape(tok, heads, clusters), 0.0), axis=2).astype(
        jnp.int32
    )
    prefix = entering(counts, "seq", lambda first, second: first + second, jnp.zeros_like(counts))

    def lookup(table):
        return jnp.sum(jnp.where(member, table.reshape(heads, clusters)[None], 0), axis=2)

    group_counts = counts.reshape(total_pairs // pairs_dev, pairs_dev)
    within = (jnp.cumsum(group_counts, axis=1) - group_counts).reshape(total_pairs)
    slot = lookup(prefix) + rank
    pair_index = jnp.arange(heads, dtype=jnp.int32)[None, :] * clusters + routes
    owner = pair_index // pairs_dev
    local_pair = pair_index % pairs_dev
    position = (owner * rows_peer + lookup(within) + rank).reshape(tok * heads)
    target = (local_pair * capacity + slot).reshape(tok * heads)
    outgoing = (
        jnp.zeros((tok * heads, width), jnp.bfloat16)
        .at[position]
        .set(qkv.reshape(tok * heads, width))
    )
    labels = jnp.zeros((tok * heads,), jnp.int32).at[position].set(target)
    arrived, places = (
        lax.all_to_all(outgoing, "seq", split_axis=0, concat_axis=0, tiled=True),
        lax.all_to_all(labels, "seq", split_axis=0, concat_axis=0, tiled=True),
    )
    tiles = jnp.zeros((pairs_dev * capacity, width), jnp.bfloat16).at[places].set(arrived)
    tiles = tiles.reshape(pairs_dev, capacity, width)
    pieces = []
    for index in range(3):
        start = index * block_rows
        stop = start + block_rows
        pieces.append(
            attend(
                tiles[:, start:stop, :head_size],
                tiles[:, :stop, head_size : 2 * head_size],
                tiles[:, :stop, 2 * head_size :],
                start,
                scale,
            )
        )
    results = jnp.concatenate(pieces, axis=1)
    flat_results = results.reshape(pairs_dev * capacity, head_size)
    replies = flat_results[places]
    returned = lax.all_to_all(replies, "seq", split_axis=0, concat_axis=0, tiled=True)
    return returned[position].reshape(tok, heads, head_size)


def solution(mesh):
    placed = (P(("groups", "seq"), None, None), P(("groups", "seq"), None))
    return jax.shard_map(
        local,
        mesh=mesh,
        in_specs=placed,
        out_specs=P(("groups", "seq"), None, None),
        check_vma=False,
    )
```

profile of v0, /device:TPU:31, one launch (start us, length us, event | category | flops | bytes accessed | tf_op | source)
XLA Modules:
  0.0 282.4 jit_solution(1487217478119262765)
XLA Ops:
  0.0 0.8 convert_reduce_fusion
  0.8 0.1 copy.13
  0.9 0.1 reshape.224
  1.0 0.1 reshape.177
  1.1 16.7 %all-gather = s32[16,1,64]{2,1,0:T(1,128)S(1)} all-gather(s32[1,1,64]{2,1,0:T(1,128)S(1)} %reshape.224), channel_id=1, replica_groups=mesh['groups'=2,'seq'=16] {'seq'}, dimensions={0}, use_global_device_ids=true | all-gather | bytes 4352 | tf_op jit(solution)/shard_map/all_gather | solution.py:13
  17.9 0.5 while.10
  18.4 0.1 broadcast_in_dim.100
  18.5 0.1 copy.19
  18.6 0.2 reduce_window_sum.13
  18.7 0.1 reduce_window_sum.14
  18.8 0.1 copy.14
  18.9 0.1 eq.32
  19.0 0.7 eq.27.clone
  19.8 0.1 compare_bitcast_fusion
  19.9 0.9 fusion.30
  20.7 0.8 select_reduce_fusion
  21.5 0.8 fusion.47
  22.4 0.1 copy.17
  22.5 0.1 reshape.178
  22.6 0.1 copy.20
  22.7 0.1 reshape.204
  22.8 16.1 %scatter_custom_fusion = s32[4096]{0:T(1024)} fusion(s32[4096]{0:T(1024)S(1)} %bitcast.33, s32[4096]{0:T(1024)S(1)} %reshape.204, s32[]{:T(128)} %constant.29.clone.1), kind=kCustom, calls=%fused_computation.84 | custom fusion | bytes 16388 | tf_op jit(solution)/shard_map/scatter | solution.py:75
  38.9 8.1 %all-to-all-start = ((s32[16,256,1]{1,2,0:T(1,128)}), s32[16,256,1]{1,2,0:T(1,128)S(1)}, u32[]{:S(2)}, u32[]{:S(2)}) async-start(s32[16,256,1]{1,2,0:T(1,128)} %bitcast.6), calls=%async_computation | async-start | bytes 32768 | tf_op jit(solution)/shard_map/all_to_all | solution.py:78
  47.0 20.5 %scatter_custom_fusion.1 = bf16[4096,384]{1,0:T(8,128)(2,1)} fusion(s32[4096]{0:T(1024)S(1)} %bitcast.34, bf16[4096,384]{1,0:T(8,128)(2,1)} %bitcast.40, bf16[]{:T(256)} %constant.27.clone.1), kind=kCustom, calls=%fused_computation.41 | custom fusion | bytes 3146240 | tf_op jit(solution)/shard_map/scatter | solution.py:73
  67.5 0.0 all-to-all-done
  67.5 6.0 %all-to-all-start.1 = ((bf16[16,256,384]{2,1,0:T(8,128)(2,1)}), bf16[16,256,384]{2,1,0:T(8,128)(2,1)S(1)}, u32[]{:S(2)}, u32[]{:S(2)}) async-start(bf16[16,256,384]{2,1,0:T(8,128)(2,1)} %bitcast.10), calls=%async_computation.1 | async-start | bytes 6291456 | tf_op jit(solution)/shard_map/all_to_all | solution.py:77
  73.5 0.1 iota_compare_fusion.2
  73.6 1.2 iota_compare_fusion.1
  74.8 1.4 iota_compare_fusion
  76.2 66.2 %all-to-all-done.1 = bf16[16,256,384]{2,1,0:T(8,128)(2,1)S(1)} async-done(((bf16[16,256,384]{2,1,0:T(8,128)(2,1)}), bf16[16,256,384]{2,1,0:T(8,128)(2,1)S(1)}, u32[]{:S(2)}, u32[]{:S(2)}) %all-to-all-start.1) | async-done | bytes 3145760 | tf_op jit(solution)/shard_map/all_to_all | solution.py:77
  142.4 21.1 %scatter_custom_fusion.2 = bf16[6144,384]{1,0:T(8,128)(2,1)} fusion(s32[4096]{0:T(1024)S(1)} %bitcast.38, bf16[4096,384]{1,0:T(8,128)(2,1)S(1)} %bitcast.31, bf16[]{:T(256)} %constant.27.clone.1), kind=kCustom, calls=%fused_computation.30 | custom fusion | bytes 4718594 | tf_op jit(solution)/shard_map/scatter | solution.py:80
  163.6 8.1 %fusion.21 = f32[4,512,1536]{2,1,0:T(8,128)} fusion(bf16[4,1536,384]{2,1,0:T(8,128)(2,1)} %bitcast.25), kind=kOutput, calls=%fused_computation.38 | convolution fusion | flops 805306368 | bytes 14680064 | tf_op jit(solution)/shard_map/pqd,pkd->pqk/dot_general | solution.py:25
  171.7 0.0 copy-done
  171.7 4.5 %fusion.32 = f32[4,512,1024]{2,1,0:T(8,128)} fusion(bf16[4,1536,384]{2,1,0:T(8,128)(2,1)S(1)} %bitcast.26), kind=kOutput, calls=%fused_computation.49 | convolution fusion | flops 536870912 | bytes 9961472 | tf_op jit(solution)/shard_map/pqd,pkd->pqk/dot_general | solution.py:25
  176.1 2.8 fusion.37
  178.9 0.0 copy-done.2
  178.9 16.0 %fusion.58 = (f32[4,512]{1,0:T(4,128)S(1)}, f32[4,512,1536]{2,1,0:T(8,128)}) fusion(f32[4,512,1536]{2,1,0:T(8,128)} %fusion.21, pred[512,1536]{1,0:T(8,128)(4,1)S(1)} %copy-done.2), kind=kOutput, calls=%fused_computation.95 | output fusion | flops 18875904 | bytes 25960448 | tf_op jit(solution)/shard_map/sub | solution.py:30
  194.9 6.6 %fusion.27 = bf16[4,512,128]{2,1,0:T(8,128)(2,1)S(1)} fusion(bf16[4,1536,384]{2,1,0:T(8,128)(2,1)S(1)} %bitcast.28, f32[4,512,1536]{2,1,0:T(8,128)} %get-tuple-element.42, f32[4,512]{1,0:T(4,128)S(1)} %get-tuple-element.41), kind=kOutput, calls=%fused_computation.45 | convolution fusion | flops 811859968 | bytes 14688256 | tf_op jit(solution)/shard_map/pqk,pkd->pqd/dot_general | solution.py:32
  201.4 0.0 copy-done.3
  201.5 13.0 %fusion.59 = (f32[4,512]{1,0:T(4,128)S(1)}, f32[4,512,1024]{2,1,0:T(8,128)}) fusion(f32[4,512,1024]{2,1,0:T(8,128)} %fusion.32, pred[512,1024]{1,0:T(8,128)(4,1)S(1)} %copy-done.3), kind=kOutput, calls=%fused_computation.96 | output fusion | flops 12583935 | bytes 17309696 | tf_op jit(solution)/shard_map/sub | solution.py:30
  214.4 4.9 %fusion.25 = bf16[4,512,128]{2,1,0:T(8,128)(2,1)S(1)} fusion(f32[4,512,1024]{2,1,0:T(8,128)} %get-tuple-element.44, f32[4,512]{1,0:T(4,128)S(1)} %get-tuple-element.43, bf16[4,1536,384]{2,1,0:T(8,128)(2,1)S(1)} %bitcast.29), kind=kOutput, calls=%fused_computation.43 | convolution fusion | flops 541327360 | bytes 9969664 | tf_op jit(solution)/shard_map/pqk,pkd->pqd/dot_general | solution.py:32
  219.3 2.1 fusion.60
  221.5 1.0 fusion.26
  222.4 0.1 pad_maximum_fusion
  222.5 15.0 %gather_fusion = bf16[4096,128]{1,0:T(8,128)(2,1)} fusion(bf16[6144,128]{1,0:T(8,128)(2,1)S(1)} %bitcast.24, s32[4096]{0:T(1024)S(1)} %broadcast_clamp_fusion.1), kind=kCustom, calls=%fused_computation | custom fusion | bytes 2113536 | tf_op jit(solution)/shard_map/gather | solution.py:97
  237.6 5.9 %all-to-all-start.2 = ((bf16[16,256,128]{2,1,0:T(8,128)(2,1)}), bf16[16,256,128]{2,1,0:T(8,128)(2,1)S(1)}, u32[]{:S(2)}, u32[]{:S(2)}) async-start(bf16[16,256,128]{2,1,0:T(8,128)(2,1)} %bitcast.14), calls=%async_computation.2 | async-start | bytes 2097152 | tf_op jit(solution)/shard_map/all_to_all | solution.py:98
  243.5 23.9 %all-to-all-done.2 = bf16[16,256,128]{2,1,0:T(8,128)(2,1)S(1)} async-done(((bf16[16,256,128]{2,1,0:T(8,128)(2,1)}), bf16[16,256,128]{2,1,0:T(8,128)(2,1)S(1)}, u32[]{:S(2)}, u32[]{:S(2)}) %all-to-all-start.2) | async-done | bytes 1048608 | tf_op jit(solution)/shard_map/all_to_all | solution.py:98
  267.4 15.0 %gather_fusion.1 = bf16[4096,128]{1,0:T(8,128)(2,1)} fusion(bf16[4096,128]{1,0:T(8,128)(2,1)S(1)} %bitcast.23, s32[4096]{0:T(1024)S(1)} %broadcast_clamp_fusion), kind=kCustom, calls=%fused_computation.1 | custom fusion | bytes 2113536 | tf_op jit(solution)/shard_map/gather | solution.py:99
  (31 shorter events, 0.3 us)
Async XLA Ops:
  38.9 28.6 %all-to-all-start = ((s32[16,256,1]{1,2,0:T(1,128)}), s32[16,256,1]{1,2,0:T(1,128)S(1)}, u32[]{:S(2)}, u32[]{:S(2)}) async-start(s32[16,256,1]{1,2,0:T(1,128)} %bitcast.6), calls=%async_computation | async-start | bytes 32768 | tf_op jit(solution)/shard_map/all_to_all | solution.py:78
  67.5 74.9 %all-to-all-start.1 = ((bf16[16,256,384]{2,1,0:T(8,128)(2,1)}), bf16[16,256,384]{2,1,0:T(8,128)(2,1)S(1)}, u32[]{:S(2)}, u32[]{:S(2)}) async-start(bf16[16,256,384]{2,1,0:T(8,128)(2,1)} %bitcast.10), calls=%async_computation.1 | async-start | bytes 6291456 | tf_op jit(solution)/shard_map/all_to_all | solution.py:77
  163.6 8.1 %copy-start = (bf16[6144,384]{1,0:T(8,128)(2,1)S(1)}, bf16[6144,384]{1,0:T(8,128)(2,1)}, u32[]{:S(2)}) copy-start(bf16[6144,384]{1,0:T(8,128)(2,1)} %scatter_custom_fusion.2) | copy-start | bytes 14155780
  176.1 2.8 copy-start.2
  194.9 6.6 %copy-start.3 = (pred[512,1024]{1,0:T(8,128)(4,1)S(1)}, pred[512,1024]{1,0:T(8,128)(4,1)}, u32[]{:S(2)}) copy-start(pred[512,1024]{1,0:T(8,128)(4,1)} %iota_compare_fusion.1) | copy-start | bytes 1572868
  214.4 4.9 %copy-start.1 = (f32[4,512,512]{1,2,0:T(8,128)S(1)}, f32[4,512,512]{1,2,0:T(8,128)}, u32[]{:S(2)}) copy-start(f32[4,512,512]{1,2,0:T(8,128)} %fusion.37) | copy-start | bytes 12582916
  237.6 29.8 %all-to-all-start.2 = ((bf16[16,256,128]{2,1,0:T(8,128)(2,1)}), bf16[16,256,128]{2,1,0:T(8,128)(2,1)S(1)}, u32[]{:S(2)}, u32[]{:S(2)}) async-start(bf16[16,256,128]{2,1,0:T(8,128)(2,1)} %bitcast.14), calls=%async_computation.2 | async-start | bytes 2097152 | tf_op jit(solution)/shard_map/all_to_all | solution.py:98
where the time goes:
time: 284 us; the launch traced here: 282 us
  waiting for transfers between devices  90.2 us (32%)
  local copies, waits for them, and re-layouts  89.7 us (32%)
  other arithmetic  36.8 us (13%)
  matrix products  28.6 us (10%)
  starting transfers between devices  20 us (7%)
  blocking collectives  16.7 us (6%)
    all_to_all x1, waiting for transfers between devices, local(): lax.all_to_all(outgoing, 'seq', split_axis=0, concat_axis=0, tiled=True)  66.2 us
    sub x3, other arithmetic, attend(): expo = jnp.exp(scores - peak)  31.1 us
    all_to_all x1, waiting for transfers between devices, local(): lax.all_to_all(replies, 'seq', split_axis=0, concat_axis=0, tiled=True)  23.9 us
    scatter x1, local copies, waits for them, and re-layouts, local(): jnp.zeros((pairs_dev * capacity, width), jnp.bfloat16).at[places]  21.1 us
    scatter x1, local copies, waits for them, and re-layouts, local(): outgoing = jnp.zeros((tok * heads, width), jnp.bfloat16).at[position].set...  20.5 us
    all_gather x1, blocking collectives, entering(): gathered = lax.all_gather(part, axis)  16.7 us
    scatter x1, local copies, waits for them, and re-layouts, local(): labels = jnp.zeros((tok * heads,), jnp.int32).at[position].set(target)  16.1 us
    dot_general x3, matrix products, attend(): jnp.einsum('pqd,pkd->pqk', queries, keys, preferred_element_type=jnp.floa...  15.3 us
  transfers between devices with their start and end apart: 3, of which 2 were waited for; matrix products, arithmetic and copies ran while one was open for 8% of the time, Pallas kernels for 0%

commit v1 on v0

--- a/solution.py
+++ b/solution.py
@@ -1,11 +1,16 @@
+import functools
 import math
 
 import jax
 import jax.numpy as jnp
 from jax import lax
+from jax.experimental import pallas as pl
+from jax.experimental.pallas import tpu as pltpu
 from jax.sharding import PartitionSpec as P
 
 CLEN = 1024
+LABEL_ROWS = 8
+NEG = -1e30
 
 
 def entering(part, axis, combine, identity):
@@ -34,7 +39,7 @@
     )
 
 
-def local(qkv, routes):
+def routed(qkv, routes):
     tok, heads, width = qkv.shape
     head_size = width // 3
     nseq = lax.axis_size("seq")
@@ -99,8 +104,215 @@
     return returned[position].reshape(tok, heads, head_size)
 
 
+def softmax_block(query, keys, values, lab_col, lab_row, scale):
+    rows, head_size = query.shape
+    span = keys.shape[0]
+    contract = (((1,), (1,)), ((), ()))
+    scores = lax.dot_general(query, keys, contract, preferred_element_type=jnp.float32)
+    same = lab_col == lab_row
+    past = span - rows
+    row_id = lax.broadcasted_iota(jnp.int32, (rows, rows), 0)
+    col_id = lax.broadcasted_iota(jnp.int32, (rows, rows), 1)
+    last = jnp.where(same[:, past:] & (col_id <= row_id), scores[:, past:], NEG)
+    if past:
+        first = jnp.where(same[:, :past], scores[:, :past], NEG)
+        scores = jnp.concatenate([first, last], axis=1)
+    else:
+        scores = last
+    factor = scale * math.log2(math.e)
+    peak = jnp.max(scores, axis=1, keepdims=True) * factor
+    expo = jnp.exp2(scores * factor - peak)
+    total = jnp.sum(expo, axis=1, keepdims=True)
+    out = jnp.dot(expo.astype(jnp.bfloat16), values, preferred_element_type=jnp.float32)
+    return (out / total).astype(jnp.bfloat16)
+
+
+def exchange_kernel(
+    nseq, held, group, x_ref, lab_ref, out_ref, recv, labs, obuf, cols,
+    x_send, x_recv, l_send, l_recv, o_send, o_recv, own_sem,
+):
+    me = lax.axis_index("seq")
+    tok, width = x_ref.shape[1:]
+    size = width // 3
+    scale = 1.0 / math.sqrt(size)
+    rows = group * tok
+
+    def peer_of(k):
+        return lax.rem(me + k, nseq)
+
+    def x_copy(j, peer):
+        return pltpu.make_async_remote_copy(
+            src_ref=x_ref.at[peer * held + j], dst_ref=recv.at[j, me],
+            send_sem=x_send.at[j, peer], recv_sem=x_recv.at[j, me],
+            device_id={"seq": peer}, device_id_type=pl.DeviceIdType.MESH,
+        )
+
+    def x_arrival(j, source):
+        return pltpu.make_async_remote_copy(
+            src_ref=x_ref.at[0], dst_ref=recv.at[j, source],
+            send_sem=x_send.at[j, source], recv_sem=x_recv.at[j, source],
+            device_id={"seq": source}, device_id_type=pl.DeviceIdType.MESH,
+        )
+
+    def l_copy(peer):
+        return pltpu.make_async_remote_copy(
+            src_ref=lab_ref.at[peer], dst_ref=labs.at[me],
+            send_sem=l_send.at[peer], recv_sem=l_recv.at[me],
+            device_id={"seq": peer}, device_id_type=pl.DeviceIdType.MESH,
+        )
+
+    def l_arrival(source):
+        return pltpu.make_async_remote_copy(
+            src_ref=lab_ref.at[0], dst_ref=labs.at[source],
+            send_sem=l_send.at[source], recv_sem=l_recv.at[source],
+            device_id={"seq": source}, device_id_type=pl.DeviceIdType.MESH,
+        )
+
+    def o_copy(j, peer):
+        return pltpu.make_async_remote_copy(
+            src_ref=obuf.at[j, peer], dst_ref=out_ref.at[me * held + j],
+            send_sem=o_send.at[j, peer], recv_sem=o_recv.at[j, me],
+            device_id={"seq": peer}, device_id_type=pl.DeviceIdType.MESH,
+        )
+
+    def o_arrival(j, source):
+        return pltpu.make_async_remote_copy(
+            src_ref=obuf.at[j, 0], dst_ref=out_ref.at[source * held + j],
+            send_sem=o_send.at[j, source], recv_sem=o_recv.at[j, source],
+            device_id={"seq": source}, device_id_type=pl.DeviceIdType.MESH,
+        )
+
+    def own_x(j):
+        return pltpu.make_async_copy(x_ref.at[me * held + j], recv.at[j, me], own_sem.at[j])
+
+    def own_o(j):
+        return pltpu.make_async_copy(
+            obuf.at[j, me], out_ref.at[me * held + j], own_sem.at[held + 1 + j]
+        )
+
+    own_l = pltpu.make_async_copy(lab_ref.at[me], labs.at[me], own_sem.at[held])
+
+    def each_peer(body):
+        def step(k, carry):
+            body(peer_of(k))
+            return carry
+
+        lax.fori_loop(1, nseq, step, 0)
+
+    own_l.start()
+    for j in range(held):
+        own_x(j).start()
+    barrier = pltpu.get_barrier_semaphore()
+    each_peer(lambda peer: pl.semaphore_signal(
+        barrier, inc=1, device_id={"seq": peer}, device_id_type=pl.DeviceIdType.MESH))
+    pl.semaphore_wait(barrier, nseq - 1)
+
+    def start_first(peer):
+        l_copy(peer).start()
+        x_copy(0, peer).start()
+
+    each_peer(start_first)
+    own_l.wait()
+    each_peer(lambda peer: l_arrival(peer).wait_recv())
+    for j in range(held):
+        own_x(j).wait()
+
+    eye = lax.broadcasted_iota(jnp.int32, (tok, tok), 0) == lax.broadcasted_iota(
+        jnp.int32, (tok, tok), 1)
+
+    for j in range(held):
+        for source in range(nseq):
+            line = labs[source, j : j + 1, :]
+            cols[j, source * tok : (source + 1) * tok, :] = jnp.sum(
+                jnp.where(eye, line, 0), axis=1, keepdims=True)
+
+    for j in range(held):
+        if j + 1 < held:
+            def forward(peer):
+                x_copy(j, peer).wait_send()
+                x_copy(j + 1, peer).start()
+
+            each_peer(forward)
+        for block in range(nseq // group):
+            sources = range(block * group, (block + 1) * group)
+            for source in sources:
+                @pl.when(me != source)
+                def _():
+                    x_arrival(j, source).wait_recv()
+            span = (block + 1) * group
+            query = recv[j, block * group : span, :, :size].reshape(rows, size)
+            keys = recv[j, :span, :, size : 2 * size].reshape(span * tok, size)
+            values = recv[j, :span, :, 2 * size :].reshape(span * tok, size)
+            lab_row = jnp.concatenate([labs[s, j : j + 1, :] for s in range(span)], axis=1)
+            lab_col = cols[j, block * rows : (block + 1) * rows, :]
+            result = softmax_block(query, keys, values, lab_col, lab_row, scale)
+            obuf[j, block * group : span] = result.reshape(group, tok, size)
+            for source in sources:
+                @pl.when(me != source)
+                def _():
+                    o_copy(j, source).start()
+
+                @pl.when(me == source)
+                def _():
+                    own_o(j).start()
+
+    each_peer(lambda peer: l_copy(peer).wait_send())
+    each_peer(lambda peer: x_copy(held - 1, peer).wait_send())
+    for j in range(held):
+        own_o(j).wait()
+
+        def finish(peer):
+            o_copy(j, peer).wait_send()
+            o_arrival(j, peer).wait_recv()
+
+        each_peer(finish)
+
+
+def by_head(qkv, routes):
+    tok, heads, width = qkv.shape
+    size = width // 3
+    nseq = lax.axis_size("seq")
+    held = heads // nseq
+    group = 2 if nseq % 2 == 0 else 1
+    lines = jnp.transpose(routes, (1, 0)).reshape(nseq, held, tok)
+    lines = jnp.pad(lines, ((0, 0), (0, LABEL_ROWS - held), (0, 0)))
+    dma = pltpu.SemaphoreType.DMA
+    out = pl.pallas_call(
+        functools.partial(exchange_kernel, nseq, held, group),
+        out_shape=jax.ShapeDtypeStruct((heads, tok, size), jnp.bfloat16),
+        in_specs=[pl.BlockSpec(memory_space=pl.ANY)] * 2,
+        out_specs=pl.BlockSpec(memory_space=pl.ANY),
+        scratch_shapes=[
+            pltpu.VMEM((held, nseq, tok, width), jnp.bfloat16),
+            pltpu.VMEM((nseq, LABEL_ROWS, tok), jnp.int32),
+            pltpu.VMEM((held, nseq, tok, size), jnp.bfloat16),
+            pltpu.VMEM((held, nseq * tok, 1), jnp.int32),
+            dma((held, nseq)),
+            dma((held, nseq)),
+            dma((nseq,)),
+            dma((nseq,)),
+            dma((held, nseq)),
+            dma((held, nseq)),
+            dma((2 * held + 1,)),
+        ],
+        compiler_params=pltpu.CompilerParams(
+            collective_id=0, has_side_effects=True, vmem_limit_bytes=48 * 2**20
+        ),
+        name="exchange",
+    )(jnp.transpose(qkv, (1, 0, 2)), lines)
+    return jnp.transpose(out, (1, 0, 2))
+
+
 def solution(mesh):
     placed = (P(("groups", "seq"), None, None), P(("groups", "seq"), None))
+    nseq = mesh.shape["seq"]
+
+    def local(qkv, routes):
+        heads = qkv.shape[1]
+        if heads % nseq == 0 and heads // nseq <= LABEL_ROWS:
+            return by_head(qkv, routes)
+        return routed(qkv, routes)
+
     return jax.shard_map(
         local,
         mesh=mesh,

time: 284 us -> 107 us (0.38)
  Pallas kernels: 0 us -> 101 us
  waiting for transfers between devices: 90.2 us -> 0 us
  local copies, waits for them, and re-layouts: 89.7 us -> 5.38 us
  other arithmetic: 36.8 us -> 0 us
  matrix products: 28.6 us -> 0 us
  starting transfers between devices: 20 us -> 0 us
  blocking collectives: 16.7 us -> 0 us
    pallas_call x0 -> x1, Pallas kernels: none -> 101 us  [by_head(): pl.pallas_call(functools.partial(exchange_kernel, nseq, held, group), out...]
    all_to_all x3 -> x0, waiting for transfers between devices: 90.2 us -> none  [the longest x1 66.2 us: local(): lax.all_to_all(outgoing, 'seq', split_axis=0, concat_axis=0, tiled=True)]
    scatter x3 -> x0, local copies, waits for them, and re-layouts: 57.8 us -> none  [the longest x1 21.1 us: local(): jnp.zeros((pairs_dev * capacity, width), jnp.bfloat16).at[places]]
    sub x4 -> x0, other arithmetic: 31.1 us -> none  [the longest x3 31.1 us: attend(): expo = jnp.exp(scores - peak)]
    gather x2 -> x0, local copies, waits for them, and re-layouts: 30.1 us -> none  [the longest x1 15 us: local(): replies = flat_results[places]]
    dot_general x7 -> x0, matrix products: 28.6 us -> none  [the longest x3 15.3 us: attend(): jnp.einsum('pqd,pkd->pqk', queries, keys, preferred_element_type=jnp.floa...]
    all_to_all x3 -> x0, starting transfers between devices: 20 us -> none  [the longest x1 8.09 us: local(): lax.all_to_all(labels, 'seq', split_axis=0, concat_axis=0, tiled=True)]
    all_gather x1 -> x0, blocking collectives: 16.7 us -> none  [entering(): gathered = lax.all_gather(part, axis)]
  transfers between devices with their start and end apart: 3 -> 0, of which waited for: 2 -> 0; matrix products, arithmetic and copies ran while one was open for 8% -> 0% of each run, Pallas kernels for 0% -> 0%
where the time goes in v1:
time: 107 us
  Pallas kernels  101 us (94%)
  local copies, waits for them, and re-layouts  5.38 us (5%)
    pallas_call x1, Pallas kernels, by_head(): pl.pallas_call(functools.partial(exchange_kernel, nseq, held, group), out...  101 us
    unnamed x1, local copies, waits for them, and re-layouts  3.01 us

profile of v1, /device:TPU:31, one launch (start us, length us, event | category | flops | bytes accessed | tf_op | source)
XLA Modules:
  0.0 106.8 jit_solution(14891487252193934178)
XLA Ops:
  0.0 0.7 pad.4.lab_ref
  0.7 3.0 %copy.6 = bf16[128,32,384]{2,0,1:T(8,128)(2,1)S(1)} copy(bf16[128,32,384]{2,1,0:T(8,128)(2,1)} %param.2) | data formatting | bytes 6291456 | tf_op args[0]
  3.7 101.4 %exchange.1 = bf16[32,128,128]{2,1,0:T(8,128)(2,1)S(1)} custom-call(bf16[32,128,384]{2,1,0:T(8,128)(2,1)S(1)} %bitcast.7, s32[16,8,128]{2,1,0:T(8,128)S(1)} %pad.4.lab_ref), custom_call_target="tpu_custom_call" | custom-call | tf_op jit(solution)/shard_map/exchange/pallas_call | solution.py:280
  105.1 1.6 %copy.4 = bf16[128,32,128]{2,1,0:T(8,128)(2,1)} copy(bf16[128,32,128]{2,0,1:T(8,128)(2,1)S(1)} %bitcast.8) | data formatting | bytes 2097152 | tf_op jit(solution)/shard_map/transpose | solution.py:303

commit v2 on v0

--- a/solution.py
+++ b/solution.py
@@ -1,11 +1,16 @@
+import functools
 import math
 
 import jax
 import jax.numpy as jnp
 from jax import lax
+from jax.experimental import pallas as pl
+from jax.experimental.pallas import tpu as pltpu
 from jax.sharding import PartitionSpec as P
 
 CLEN = 1024
+LABEL_ROWS = 8
+NEG = -1e30
 
 
 def entering(part, axis, combine, identity):
@@ -34,7 +39,7 @@
     )
 
 
-def local(qkv, routes):
+def routed(qkv, routes):
     tok, heads, width = qkv.shape
     head_size = width // 3
     nseq = lax.axis_size("seq")
@@ -99,8 +104,384 @@
     return returned[position].reshape(tok, heads, head_size)
 
 
+def partial_softmax(query, keys, values, lab_col, lab_row, scale, causal):
+    rows, head_size = query.shape
+    span = keys.shape[0]
+    contract = (((1,), (1,)), ((), ()))
+    scores = lax.dot_general(query, keys, contract, preferred_element_type=jnp.float32)
+    same = lab_col == lab_row
+    if causal:
+        past = span - rows
+        row_id = lax.broadcasted_iota(jnp.int32, (rows, rows), 0)
+        col_id = lax.broadcasted_iota(jnp.int32, (rows, rows), 1)
+        last = jnp.where(same[:, past:] & (col_id <= row_id), scores[:, past:], NEG)
+        if past:
+            first = jnp.where(same[:, :past], scores[:, :past], NEG)
+            scores = jnp.concatenate([first, last], axis=1)
+        else:
+            scores = last
+    else:
+        scores = jnp.where(same, scores, NEG)
+    factor = scale * math.log2(math.e)
+    peak = jnp.max(scores, axis=1, keepdims=True) * factor
+    expo = jnp.exp2(scores * factor - peak)
+    total = jnp.sum(expo, axis=1, keepdims=True)
+    out = jnp.dot(expo.astype(jnp.bfloat16), values, preferred_element_type=jnp.float32)
+    return (out / total).astype(jnp.bfloat16), peak, total
+
+
+def exchange_kernel(
+    nseq, held, group, x_ref, lab_ref, out_ref, recv, qrecv, labs, obuf, sbuf, part, stats, merged, cols,
+    x_send, x_recv, q_send, q_recv, l_send, l_recv, o_send, o_recv, s_send, s_recv,
+    own_x, own_l, own_o, own_s, m_sem,
+):
+    me = lax.axis_index("seq")
+    half = nseq // 2
+    low = me < half
+    up = me >= half
+    side = me // half
+    base = side * half
+    mine = lax.rem(me, half)
+    tok, width = x_ref.shape[1:]
+    size = width // 3
+    scale = 1.0 / math.sqrt(size)
+    rows = group * tok
+
+    def remote(src, dst, send, recv_sem, peer):
+        return pltpu.make_async_remote_copy(
+            src_ref=src, dst_ref=dst, send_sem=send, recv_sem=recv_sem,
+            device_id={"seq": peer}, device_id_type=pl.DeviceIdType.MESH,
+        )
+
+    def x_copy(j, p):
+        return remote(x_ref.at[p * held + j], recv.at[j, mine],
+                      x_send.at[j, p], x_recv.at[j, mine], base + p)
+
+    def x_arrival(j, p):
+        return remote(x_ref.at[0], recv.at[j, p], x_send.at[j, p], x_recv.at[j, p], base + p)
+
+    def q_copy(j, p):
+        return remote(x_ref.at[p * held + j, :, pl.ds(0, size)], qrecv.at[j, mine],
+                      q_send.at[j, p], q_recv.at[j, mine], p)
+
+    def q_arrival(j, p):
+        return remote(x_ref.at[0, :, pl.ds(0, size)], qrecv.at[j, p],
+                      q_send.at[j, p], q_recv.at[j, p], half + p)
+
+    def l_copy(peer):
+        return remote(lab_ref.at[lax.rem(peer, half)], labs.at[me],
+                      l_send.at[peer], l_recv.at[me], peer)
+
+    def l_arrival(peer):
+        return remote(lab_ref.at[0], labs.at[peer], l_send.at[peer], l_recv.at[peer], peer)
+
+    def o_copy_low(j, p):
+        return remote(obuf.at[j, p], out_ref.at[mine * held + j],
+                      o_send.at[j, p], o_recv.at[0, j, mine], p)
+
+    def o_arrival_low(j, p):
+        return remote(obuf.at[j, 0], out_ref.at[p * held + j],
+                      o_send.at[j, p], o_recv.at[0, j, p], p)
+
+    def o_copy_up(j, peer):
+        return remote(obuf.at[j, peer], part.at[side, mine * held + j],
+                      o_send.at[j, peer], o_recv.at[side, j, mine], peer)
+
+    def o_arrival_up(which, j, p):
+        return remote(obuf.at[j, 0], part.at[which, p * held + j],
+                      o_send.at[j, which * half + p], o_recv.at[which, j, p], which * half + p)
+
+    def s_copy(j, peer):
+        return remote(sbuf.at[j, peer], stats.at[side, mine, j],
+                      s_send.at[j, peer], s_recv.at[side, j, mine], peer)
+
+    def s_arrival(which, j, p):
+        return remote(sbuf.at[j, 0], stats.at[which, p, j],
+                      s_send.at[j, which * half + p], s_recv.at[which, j, p], which * half + p)
+
+    def own_x_copy(j):
+        return pltpu.make_async_copy(x_ref.at[mine * held + j], recv.at[j, mine], own_x.at[j])
+
+    def own_o_low(j):
+        return pltpu.make_async_copy(obuf.at[j, me], out_ref.at[mine * held + j], own_o.at[j])
+
+    def own_o_up(j):
+        return pltpu.make_async_copy(obuf.at[j, me], part.at[1, mine * held + j], own_o.at[j])
+
+    def own_s_up(j):
+        return pltpu.make_async_copy(sbuf.at[j, me], stats.at[1, mine, j], own_s.at[j])
+
+    def result_copy(head):
+        return pltpu.make_async_copy(merged.at[head], out_ref.at[head], m_sem.at[head])
+
+    own_lab = pltpu.make_async_copy(lab_ref.at[mine], labs.at[me], own_l.at[0])
+
+    def loop(start, stop, body):
+        def step(k, carry):
+            body(k)
+            return carry
+
+        lax.fori_loop(start, stop, step, 0)
+
+    def each_peer(body):
+        loop(1, nseq, lambda k: body(lax.rem(me + k, nseq)))
+
+    def each_near(body):
+        loop(1, half, lambda k: body(lax.rem(mine + k, half)))
+
+    def each_far(body):
+        loop(0, half, lambda k: body(lax.rem(mine + k, half)))
+
+    own_lab.start()
+    for j in range(held):
+        own_x_copy(j).start()
+    barrier = pltpu.get_barrier_semaphore()
+    each_peer(lambda peer: pl.semaphore_signal(
+        barrier, inc=1, device_id={"seq": peer}, device_id_type=pl.DeviceIdType.MESH))
+    pl.semaphore_wait(barrier, nseq - 1)
+
+    each_near(lambda p: l_copy(base + p).start())
+
+    @pl.when(up)
+    def _():
+        each_far(lambda p: l_copy(p).start())
+        each_far(lambda p: q_copy(0, p).start())
+
+    each_near(lambda p: x_copy(0, p).start())
+    own_lab.wait()
+    for j in range(held):
+        own_x_copy(j).wait()
+    each_near(lambda p: l_arrival(base + p).wait_recv())
+
+    @pl.when(low)
+    def _():
+        each_far(lambda p: l_arrival(half + p).wait_recv())
+
+    eye = lax.broadcasted_iota(jnp.int32, (tok, tok), 0) == lax.broadcasted_iota(
+        jnp.int32, (tok, tok), 1)
+
+    def to_col(line):
+        return jnp.sum(jnp.where(eye, line, jnp.zeros_like(line)), axis=1, keepdims=True)
+
+    def to_row(col):
+        return jnp.sum(jnp.where(eye, col, jnp.zeros_like(col)), axis=0, keepdims=True)
+
+    def keep(j, first, block, result, peak, total):
+        for g in range(group):
+            source = first + block * group + g
+            obuf[j, source] = result[g * tok : (g + 1) * tok]
+            sbuf[j, source, 0:1, :] = to_row(peak[g * tok : (g + 1) * tok])
+            sbuf[j, source, 1:2, :] = to_row(total[g * tok : (g + 1) * tok])
+
+    def chunk(j):
+        @pl.when(j + 1 < held)
+        def _():
+            @pl.when(up)
+            def _():
+                def forward_q(p):
+                    q_copy(j, p).wait_send()
+                    q_copy(j + 1, p).start()
+
+                each_far(forward_q)
+
+            def forward_x(p):
+                x_copy(j, p).wait_send()
+                x_copy(j + 1, p).start()
+
+            each_near(forward_x)
+
+        def fill_cols(p):
+            cols[base + p] = to_col(labs[base + p, pl.ds(j, 1), :])
+
+        loop(0, half, fill_cols)
+
+        @pl.when(low)
+        def _():
+            def fill_far(p):
+                cols[half + p] = to_col(labs[half + p, pl.ds(j, 1), :])
+
+            loop(0, half, fill_far)
+
+        for block in range(half // group):
+            for g in range(group):
+                p = block * group + g
+
+                @pl.when(mine != p)
+                def _():
+                    x_arrival(j, p).wait_recv()
+
+            span = (block + 1) * group
+            query = recv[j, block * group : span, :, :size].reshape(rows, size)
+            keys = recv[j, :span, :, size : 2 * size].reshape(span * tok, size)
+            values = recv[j, :span, :, 2 * size :].reshape(span * tok, size)
+            lab_row = jnp.concatenate(
+                [labs[base + p, pl.ds(j, 1), :] for p in range(span)], axis=1)
+            lab_col = jnp.concatenate(
+                [cols[base + block * group + g] for g in range(group)], axis=0)
+            result, peak, total = partial_softmax(
+                query, keys, values, lab_col, lab_row, scale, True)
+            keep(j, base, block, result, peak, total)
+            for g in range(group):
+                p = block * group + g
+
+                @pl.when(low & (mine != p))
+                def _():
+                    o_copy_low(j, p).start()
+
+                @pl.when(low & (mine == p))
+                def _():
+                    own_o_low(j).start()
+
+                @pl.when(up & (mine != p))
+                def _():
+                    o_copy_up(j, half + p).start()
+                    s_copy(j, half + p).start()
+
+                @pl.when(up & (mine == p))
+                def _():
+                    own_o_up(j).start()
+                    own_s_up(j).start()
+
+        @pl.when(low)
+        def _():
+            for block in range(half // group):
+                for g in range(group):
+                    q_arrival(j, block * group + g).wait_recv()
+                query = qrecv[j, block * group : (block + 1) * group].reshape(rows, size)
+                keys = recv[j, :, :, size : 2 * size].reshape(half * tok, size)
+                values = recv[j, :, :, 2 * size :].reshape(half * tok, size)
+                lab_row = jnp.concatenate(
+                    [labs[p, pl.ds(j, 1), :] for p in range(half)], axis=1)
+                lab_col = jnp.concatenate(
+                    [cols[half + block * group + g] for g in range(group)], axis=0)
+                result, peak, total = partial_softmax(
+                    query, keys, values, lab_col, lab_row, scale, False)
+                keep(j, half, block, result, peak, total)
+                for g in range(group):
+                    o_copy_up(j, half + block * group + g).start()
+                    s_copy(j, half + block * group + g).start()
+
+    loop(0, held, chunk)
+
+    each_near(lambda p: l_copy(base + p).wait_send())
+    each_near(lambda p: x_copy(held - 1, p).wait_send())
+
+    @pl.when(low)
+    def _():
+        def finish(j):
+            own_o_low(j).wait()
+
+            def near(p):
+                o_copy_low(j, p).wait_send()
+                o_arrival_low(j, p).wait_recv()
+
+            def far(p):
+                o_copy_up(j, half + p).wait_send()
+                s_copy(j, half + p).wait_send()
+
+            each_near(near)
+            each_far(far)
+
+        loop(0, held, finish)
+
+    @pl.when(up)
+    def _():
+        each_far(lambda p: l_copy(p).wait_send())
+        each_far(lambda p: q_copy(held - 1, p).wait_send())
+
+        def finish(j):
+            own_o_up(j).wait()
+            own_s_up(j).wait()
+
+            def near(p):
+                o_copy_up(j, half + p).wait_send()
+                s_copy(j, half + p).wait_send()
+                o_arrival_up(1, j, p).wait_recv()
+                s_arrival(1, j, p).wait_recv()
+
+            each_near(near)
+
+            def merge(p):
+                o_arrival_up(0, j, p).wait_recv()
+                s_arrival(0, j, p).wait_recv()
+                head = p * held + j
+                peak0, peak1 = stats[0, p, j, 0:1, :], stats[1, p, j, 0:1, :]
+                peak = jnp.maximum(peak0, peak1)
+                weight0 = stats[0, p, j, 1:2, :] * jnp.exp2(peak0 - peak)
+                weight1 = stats[1, p, j, 1:2, :] * jnp.exp2(peak1 - peak)
+                total = weight0 + weight1
+                merged[head] = (
+                    to_col(weight0 / total) * part[0, head].astype(jnp.float32)
+                    + to_col(weight1 / total) * part[1, head].astype(jnp.float32)
+                ).astype(jnp.bfloat16)
+                result_copy(head).start()
+
+            loop(0, half, merge)
+
+        loop(0, held, finish)
+        loop(0, half * held, lambda head: result_copy(head).wait())
+
+
+def by_head(qkv, routes):
+    tok, heads, width = qkv.shape
+    size = width // 3
+    nseq = lax.axis_size("seq")
+    half = nseq // 2
+    held = heads // half
+    group = 2 if half % 2 == 0 else 1
+    lines = jnp.transpose(routes, (1, 0)).reshape(half, held, tok)
+    lines = jnp.pad(lines, ((0, 0), (0, LABEL_ROWS - held), (0, 0)))
+    dma = pltpu.SemaphoreType.DMA
+    out = pl.pallas_call(
+        functools.partial(exchange_kernel, nseq, held, group),
+        out_shape=jax.ShapeDtypeStruct((heads, tok, size), jnp.bfloat16),
+        in_specs=[pl.BlockSpec(memory_space=pl.ANY)] * 2,
+        out_specs=pl.BlockSpec(memory_space=pl.ANY),
+        scratch_shapes=[
+            pltpu.VMEM((held, half, tok, width), jnp.bfloat16),
+            pltpu.VMEM((held, half, tok, size), jnp.bfloat16),
+            pltpu.VMEM((nseq, LABEL_ROWS, tok), jnp.int32),
+            pltpu.VMEM((held, nseq, tok, size), jnp.bfloat16),
+            pltpu.VMEM((held, nseq, 8, tok), jnp.float32),
+            pltpu.VMEM((2, heads, tok, size), jnp.bfloat16),
+            pltpu.VMEM((2, half, held, 8, tok), jnp.float32),
+            pltpu.VMEM((heads, tok, size), jnp.bfloat16),
+            pltpu.VMEM((nseq, tok, 1), jnp.int32),
+            dma((held, half)),
+            dma((held, half)),
+            dma((held, half)),
+            dma((held, half)),
+            dma((nseq,)),
+            dma((nseq,)),
+            dma((held, nseq)),
+            dma((2, held, half)),
+            dma((held, nseq)),
+            dma((2, held, half)),
+            dma((held,)),
+            dma((1,)),
+            dma((held,)),
+            dma((held,)),
+            dma((heads,)),
+        ],
+        compiler_params=pltpu.CompilerParams(
+            collective_id=0, has_side_effects=True, vmem_limit_bytes=48 * 2**20
+        ),
+        name="exchange",
+    )(jnp.transpose(qkv, (1, 0, 2)), lines)
+    return jnp.transpose(out, (1, 0, 2))
+
+
 def solution(mesh):
     placed = (P(("groups", "seq"), None, None), P(("groups", "seq"), None))
+    nseq = mesh.shape["seq"]
+
+    def local(qkv, routes):
+        heads = qkv.shape[1]
+        half = nseq // 2
+        if nseq % 2 == 0 and heads % half == 0 and heads // half <= LABEL_ROWS:
+            return by_head(qkv, routes)
+        return routed(qkv, routes)
+
     return jax.shard_map(
         local,
         mesh=mesh,

time: 284 us -> 95.7 us (0.34)
  waiting for transfers between devices: 90.2 us -> 0 us
  Pallas kernels: 0 us -> 90.1 us
  local copies, waits for them, and re-layouts: 89.7 us -> 5.38 us
  other arithmetic: 36.8 us -> 0 us
  matrix products: 28.6 us -> 0 us
  starting transfers between devices: 20 us -> 0 us
  blocking collectives: 16.7 us -> 0 us
    all_to_all x3 -> x0, waiting for transfers between devices: 90.2 us -> none  [the longest x1 66.2 us: local(): lax.all_to_all(outgoing, 'seq', split_axis=0, concat_axis=0, tiled=True)]
    pallas_call x0 -> x1, Pallas kernels: none -> 90.1 us  [by_head(): pl.pallas_call(functools.partial(exchange_kernel, nseq, held, group), out...]
    scatter x3 -> x0, local copies, waits for them, and re-layouts: 57.8 us -> none  [the longest x1 21.1 us: local(): jnp.zeros((pairs_dev * capacity, width), jnp.bfloat16).at[places]]
    sub x4 -> x0, other arithmetic: 31.1 us -> none  [the longest x3 31.1 us: attend(): expo = jnp.exp(scores - peak)]
    gather x2 -> x0, local copies, waits for them, and re-layouts: 30.1 us -> none  [the longest x1 15 us: local(): replies = flat_results[places]]
    dot_general x7 -> x0, matrix products: 28.6 us -> none  [the longest x3 15.3 us: attend(): jnp.einsum('pqd,pkd->pqk', queries, keys, preferred_element_type=jnp.floa...]
    all_to_all x3 -> x0, starting transfers between devices: 20 us -> none  [the longest x1 8.09 us: local(): lax.all_to_all(labels, 'seq', split_axis=0, concat_axis=0, tiled=True)]
    all_gather x1 -> x0, blocking collectives: 16.7 us -> none  [entering(): gathered = lax.all_gather(part, axis)]
  transfers between devices with their start and end apart: 3 -> 0, of which waited for: 2 -> 0; matrix products, arithmetic and copies ran while one was open for 8% -> 0% of each run, Pallas kernels for 0% -> 0%
where the time goes in v2:
time: 95.7 us; the launch traced here: 95.5 us
  Pallas kernels  90.1 us (94%)
  local copies, waits for them, and re-layouts  5.38 us (6%)
    pallas_call x1, Pallas kernels, by_head(): pl.pallas_call(functools.partial(exchange_kernel, nseq, held, group), out...  90.1 us
    unnamed x1, local copies, waits for them, and re-layouts  3.01 us

profile of v2, /device:TPU:31, one launch (start us, length us, event | category | flops | bytes accessed | tf_op | source)
XLA Modules:
  0.0 95.5 jit_solution(15246006173781627753)
XLA Ops:
  0.0 0.7 pad.4.lab_ref
  0.7 3.0 %copy.6 = bf16[128,32,384]{2,0,1:T(8,128)(2,1)S(1)} copy(bf16[128,32,384]{2,1,0:T(8,128)(2,1)} %param.2) | data formatting | bytes 6291456 | tf_op args[0]
  3.7 90.1 %exchange.1 = bf16[32,128,128]{2,1,0:T(8,128)(2,1)S(1)} custom-call(bf16[32,128,384]{2,1,0:T(8,128)(2,1)S(1)} %bitcast.7, s32[8,8,128]{2,1,0:T(8,128)S(1)} %pad.4.lab_ref), custom_call_target="tpu_custom_call" | custom-call | tf_op jit(solution)/shard_map/exchange/pallas_call | solution.py:435
  93.8 1.6 %copy.4 = bf16[128,32,128]{2,1,0:T(8,128)(2,1)} copy(bf16[128,32,128]{2,0,1:T(8,128)(2,1)S(1)} %bitcast.8) | data formatting | bytes 2097152 | tf_op jit(solution)/shard_map/transpose | solution.py:471

commit v3 on v2

--- a/solution.py
+++ b/solution.py
@@ -245,9 +245,15 @@
     @pl.when(up)
     def _():
         each_far(lambda p: l_copy(p).start())
-        each_far(lambda p: q_copy(0, p).start())
-
-    each_near(lambda p: x_copy(0, p).start())
+
+    def send_chunk(j):
+        @pl.when(up)
+        def _():
+            each_far(lambda p: q_copy(j, p).start())
+
+        each_near(lambda p: x_copy(j, p).start())
+
+    loop(0, held, send_chunk)
     own_lab.wait()
     for j in range(held):
         own_x_copy(j).wait()
@@ -274,22 +280,6 @@
             sbuf[j, source, 1:2, :] = to_row(total[g * tok : (g + 1) * tok])
 
     def chunk(j):
-        @pl.when(j + 1 < held)
-        def _():
-            @pl.when(up)
-            def _():
-                def forward_q(p):
-                    q_copy(j, p).wait_send()
-                    q_copy(j + 1, p).start()
-
-                each_far(forward_q)
-
-            def forward_x(p):
-                x_copy(j, p).wait_send()
-                x_copy(j + 1, p).start()
-
-            each_near(forward_x)
-
         def fill_cols(p):
             cols[base + p] = to_col(labs[base + p, pl.ds(j, 1), :])
 
@@ -364,7 +354,7 @@
     loop(0, held, chunk)
 
     each_near(lambda p: l_copy(base + p).wait_send())
-    each_near(lambda p: x_copy(held - 1, p).wait_send())
+    loop(0, held, lambda j: each_near(lambda p: x_copy(j, p).wait_send()))
 
     @pl.when(low)
     def _():
@@ -387,7 +377,7 @@
     @pl.when(up)
     def _():
         each_far(lambda p: l_copy(p).wait_send())
-        each_far(lambda p: q_copy(held - 1, p).wait_send())
+        loop(0, held, lambda j: each_far(lambda p: q_copy(j, p).wait_send()))
 
         def finish(j):
             own_o_up(j).wait()

time: 95.7 us -> 94.2 us (0.984)
  Pallas kernels: 90.1 us -> 88.6 us
    pallas_call x1, Pallas kernels: 90.1 us -> 88.6 us  [by_head(): pl.pallas_call(functools.partial(exchange_kernel, nseq, held, group), out...]
where the time goes in v3:
time: 94.2 us; the launch traced here: 94 us
  Pallas kernels  88.6 us (94%)
  local copies, waits for them, and re-layouts  5.38 us (6%)
    pallas_call x1, Pallas kernels, by_head(): pl.pallas_call(functools.partial(exchange_kernel, nseq, held, group), out...  88.6 us
    unnamed x1, local copies, waits for them, and re-layouts  3.01 us

profile of v3, /device:TPU:31, one launch (start us, length us, event | category | flops | bytes accessed | tf_op | source)
XLA Modules:
  0.0 94.0 jit_solution(5875751594158560457)
XLA Ops:
  0.0 0.7 pad.4.lab_ref
  0.7 3.0 %copy.6 = bf16[128,32,384]{2,0,1:T(8,128)(2,1)S(1)} copy(bf16[128,32,384]{2,1,0:T(8,128)(2,1)} %param.2) | data formatting | bytes 6291456 | tf_op args[0]
  3.7 88.6 %exchange.1 = bf16[32,128,128]{2,1,0:T(8,128)(2,1)S(1)} custom-call(bf16[32,128,384]{2,1,0:T(8,128)(2,1)S(1)} %bitcast.7, s32[8,8,128]{2,1,0:T(8,128)S(1)} %pad.4.lab_ref), custom_call_target="tpu_custom_call" | custom-call | tf_op jit(solution)/shard_map/exchange/pallas_call | solution.py:425
  92.3 1.6 %copy.4 = bf16[128,32,128]{2,1,0:T(8,128)(2,1)} copy(bf16[128,32,128]{2,0,1:T(8,128)(2,1)S(1)} %bitcast.8) | data formatting | bytes 2097152 | tf_op jit(solution)/shard_map/transpose | solution.py:461

commit v4 on v3

--- a/solution.py
+++ b/solution.py
@@ -10,7 +10,7 @@
 
 CLEN = 1024
 LABEL_ROWS = 8
-NEG = -1e30
+NEG = -1e36
 
 
 def entering(part, axis, combine, identity):
@@ -104,34 +104,28 @@
     return returned[position].reshape(tok, heads, head_size)
 
 
-def partial_softmax(query, keys, values, lab_col, lab_row, scale, causal):
-    rows, head_size = query.shape
+def partial_softmax(query, keys, values, scale, causal):
+    rows = query.shape[0]
     span = keys.shape[0]
+    size = values.shape[1] // 2
     contract = (((1,), (1,)), ((), ()))
     scores = lax.dot_general(query, keys, contract, preferred_element_type=jnp.float32)
-    same = lab_col == lab_row
     if causal:
         past = span - rows
         row_id = lax.broadcasted_iota(jnp.int32, (rows, rows), 0)
         col_id = lax.broadcasted_iota(jnp.int32, (rows, rows), 1)
-        last = jnp.where(same[:, past:] & (col_id <= row_id), scores[:, past:], NEG)
-        if past:
-            first = jnp.where(same[:, :past], scores[:, :past], NEG)
-            scores = jnp.concatenate([first, last], axis=1)
-        else:
-            scores = last
-    else:
-        scores = jnp.where(same, scores, NEG)
+        last = jnp.where(col_id <= row_id, scores[:, past:], NEG)
+        scores = jnp.concatenate([scores[:, :past], last], axis=1) if past else last
     factor = scale * math.log2(math.e)
     peak = jnp.max(scores, axis=1, keepdims=True) * factor
-    expo = jnp.exp2(scores * factor - peak)
-    total = jnp.sum(expo, axis=1, keepdims=True)
-    out = jnp.dot(expo.astype(jnp.bfloat16), values, preferred_element_type=jnp.float32)
-    return (out / total).astype(jnp.bfloat16), peak, total
+    expo = jnp.exp2(scores * factor - peak).astype(jnp.bfloat16)
+    out = jnp.dot(expo, values, preferred_element_type=jnp.float32)
+    total = out[:, size:]
+    return (out[:, :size] / total).astype(jnp.bfloat16), peak, total[:, :1]
 
 
 def exchange_kernel(
-    nseq, held, group, x_ref, lab_ref, out_ref, recv, qrecv, labs, obuf, sbuf, part, stats, merged, cols,
+    nseq, held, group, x_ref, lab_ref, out_ref, recv, qrecv, labs, obuf, sbuf, part, stats, merged, hot, cold,
     x_send, x_recv, q_send, q_recv, l_send, l_recv, o_send, o_recv, s_send, s_recv,
     own_x, own_l, own_o, own_s, m_sem,
 ):
@@ -146,6 +140,7 @@
     size = width // 3
     scale = 1.0 / math.sqrt(size)
     rows = group * tok
+    wide = 2 * group if half % (2 * group) == 0 else group
 
     def remote(src, dst, send, recv_sem, peer):
         return pltpu.make_async_remote_copy(
@@ -272,84 +267,74 @@
     def to_row(col):
         return jnp.sum(jnp.where(eye, col, jnp.zeros_like(col)), axis=0, keepdims=True)
 
-    def keep(j, first, block, result, peak, total):
-        for g in range(group):
-            source = first + block * group + g
-            obuf[j, source] = result[g * tok : (g + 1) * tok]
-            sbuf[j, source, 0:1, :] = to_row(peak[g * tok : (g + 1) * tok])
-            sbuf[j, source, 1:2, :] = to_row(total[g * tok : (g + 1) * tok])
+    def keep(j, first, count, result, peak, total):
+        for g in range(count):
+            part_rows = slice(g * tok, (g + 1) * tok)
+            obuf[j, first + g] = result[part_rows]
+            sbuf[j, first + g, 0:1, :] = to_row(peak[part_rows])
+            sbuf[j, first + g, 1:2, :] = to_row(total[part_rows])
 
     def chunk(j):
-        def fill_cols(p):
-            cols[base + p] = to_col(labs[base + p, pl.ds(j, 1), :])
-
-        loop(0, half, fill_cols)
+        def label_match(source):
+            col = to_col(labs[source, pl.ds(j, 1), :])
+            return lax.broadcasted_iota(jnp.int32, (tok, size), 1) == col
+
+        def fill_near(p):
+            match = label_match(base + p)
+            hot[base + p] = jnp.where(match, 1.0, 0.0).astype(jnp.bfloat16)
+            cold[p] = jnp.where(match, 0.0, NEG).astype(jnp.bfloat16)
+
+        loop(0, half, fill_near)
+        each_near(lambda p: x_arrival(j, p).wait_recv())
+
+        def keys_of(span):
+            keys = recv[j, :span, :, size : 2 * size].reshape(span * tok, size)
+            return jnp.concatenate([keys, cold[:span].reshape(span * tok, size)], axis=1)
+
+        def values_of(span):
+            values = recv[j, :span, :, 2 * size :].reshape(span * tok, size)
+            return jnp.concatenate([values, jnp.ones((span * tok, size), jnp.bfloat16)], axis=1)
 
         @pl.when(low)
         def _():
             def fill_far(p):
-                cols[half + p] = to_col(labs[half + p, pl.ds(j, 1), :])
+                hot[half + p] = jnp.where(label_match(half + p), 1.0, 0.0).astype(jnp.bfloat16)
 
             loop(0, half, fill_far)
-
-        for block in range(half // group):
-            for g in range(group):
-                p = block * group + g
-
-                @pl.when(mine != p)
-                def _():
-                    x_arrival(j, p).wait_recv()
-
-            span = (block + 1) * group
-            query = recv[j, block * group : span, :, :size].reshape(rows, size)
-            keys = recv[j, :span, :, size : 2 * size].reshape(span * tok, size)
-            values = recv[j, :span, :, 2 * size :].reshape(span * tok, size)
-            lab_row = jnp.concatenate(
-                [labs[base + p, pl.ds(j, 1), :] for p in range(span)], axis=1)
-            lab_col = jnp.concatenate(
-                [cols[base + block * group + g] for g in range(group)], axis=0)
+            each_far(lambda p: q_arrival(j, p).wait_recv())
+            for first in range(0, half, wide):
+                query = jnp.concatenate([
+                    qrecv[j, first : first + wide].reshape(wide * tok, size),
+                    hot[half + first : half + first + wide].reshape(wide * tok, size)], axis=1)
+                result, peak, total = partial_softmax(
+                    query, keys_of(half), values_of(half), scale, False)
+                keep(j, half + first, wide, result, peak, total)
+                for g in range(wide):
+                    o_copy_up(j, half + first + g).start()
+                    s_copy(j, half + first + g).start()
+
+        for first in range(0, half, group):
+            query = jnp.concatenate([
+                recv[j, first : first + group, :, :size].reshape(rows, size),
+                hot[pl.ds(base + first, group)].reshape(rows, size)], axis=1)
             result, peak, total = partial_softmax(
-                query, keys, values, lab_col, lab_row, scale, True)
-            keep(j, base, block, result, peak, total)
-            for g in range(group):
-                p = block * group + g
-
-                @pl.when(low & (mine != p))
-                def _():
-                    o_copy_low(j, p).start()
-
-                @pl.when(low & (mine == p))
-                def _():
-                    own_o_low(j).start()
-
-                @pl.when(up & (mine != p))
-                def _():
-                    o_copy_up(j, half + p).start()
-                    s_copy(j, half + p).start()
-
-                @pl.when(up & (mine == p))
-                def _():
-                    own_o_up(j).start()
-                    own_s_up(j).start()
+                query, keys_of(first + group), values_of(first + group), scale, True)
+            keep(j, base + first, group, result, peak, total)
 
         @pl.when(low)
         def _():
-            for block in range(half // group):
-                for g in range(group):
-                    q_arrival(j, block * group + g).wait_recv()
-                query = qrecv[j, block * group : (block + 1) * group].reshape(rows, size)
-                keys = recv[j, :, :, size : 2 * size].reshape(half * tok, size)
-                values = recv[j, :, :, 2 * size :].reshape(half * tok, size)
-                lab_row = jnp.concatenate(
-                    [labs[p, pl.ds(j, 1), :] for p in range(half)], axis=1)
-                lab_col = jnp.concatenate(
-                    [cols[half + block * group + g] for g in range(group)], axis=0)
-                result, peak, total = partial_softmax(
-                    query, keys, values, lab_col, lab_row, scale, False)
-                keep(j, half, block, result, peak, total)
-                for g in range(group):
-                    o_copy_up(j, half + block * group + g).start()
-                    s_copy(j, half + block * group + g).start()
+            each_near(lambda p: o_copy_low(j, p).start())
+            own_o_low(j).start()
+
+        @pl.when(up)
+        def _():
+            def send_up(p):
+                o_copy_up(j, half + p).start()
+                s_copy(j, half + p).start()
+
+            each_near(send_up)
+            own_o_up(j).start()
+            own_s_up(j).start()
 
     loop(0, held, chunk)
 
@@ -436,7 +421,8 @@
             pltpu.VMEM((2, heads, tok, size), jnp.bfloat16),
             pltpu.VMEM((2, half, held, 8, tok), jnp.float32),
             pltpu.VMEM((heads, tok, size), jnp.bfloat16),
-            pltpu.VMEM((nseq, tok, 1), jnp.int32),
+            pltpu.VMEM((nseq, tok, size), jnp.bfloat16),
+            pltpu.VMEM((half, tok, size), jnp.bfloat16),
             dma((held, half)),
             dma((held, half)),
             dma((held, half)),
@@ -468,7 +454,9 @@
     def local(qkv, routes):
         heads = qkv.shape[1]
         half = nseq // 2
-        if nseq % 2 == 0 and heads % half == 0 and heads // half <= LABEL_ROWS:
+        clusters = nseq * qkv.shape[0] // CLEN
+        fits = clusters <= qkv.shape[2] // 3
+        if fits and nseq % 2 == 0 and heads % half == 0 and heads // half <= LABEL_ROWS:
             return by_head(qkv, routes)
         return routed(qkv, routes)
 

time: 94.2 us -> 93.4 us (level)
  no operation moved by 1% of the time
where the time goes in v4:
time: 93.4 us; the launch traced here: 93.2 us
  Pallas kernels  87.8 us (94%)
  local copies, waits for them, and re-layouts  5.38 us (6%)
    pallas_call x1, Pallas kernels, by_head(): pl.pallas_call(functools.partial(exchange_kernel, nseq, held, group), out...  87.8 us
    unnamed x1, local copies, waits for them, and re-layouts  3.01 us

profile of v4, /device:TPU:31, one launch (start us, length us, event | category | flops | bytes accessed | tf_op | source)
XLA Modules:
  0.0 93.2 jit_solution(7765682600509625339)
XLA Ops:
  0.0 0.7 pad.4.lab_ref
  0.7 3.0 %copy.6 = bf16[128,32,384]{2,0,1:T(8,128)(2,1)S(1)} copy(bf16[128,32,384]{2,1,0:T(8,128)(2,1)} %param.2) | data formatting | bytes 6291456 | tf_op args[0]
  3.7 87.8 %exchange.1 = bf16[32,128,128]{2,1,0:T(8,128)(2,1)S(1)} custom-call(bf16[32,128,384]{2,1,0:T(8,128)(2,1)S(1)} %bitcast.7, s32[8,8,128]{2,1,0:T(8,128)S(1)} %pad.4.lab_ref), custom_call_target="tpu_custom_call" | custom-call | tf_op jit(solution)/shard_map/exchange/pallas_call | solution.py:410
  91.5 1.6 %copy.4 = bf16[128,32,128]{2,1,0:T(8,128)(2,1)} copy(bf16[128,32,128]{2,0,1:T(8,128)(2,1)S(1)} %bitcast.8) | data formatting | bytes 2097152 | tf_op jit(solution)/shard_map/transpose | solution.py:447

commit v5 on v4

--- a/solution.py
+++ b/solution.py
@@ -140,6 +140,7 @@
     size = width // 3
     scale = 1.0 / math.sqrt(size)
     rows = group * tok
+    ahead = 2
     wide = 2 * group if half % (2 * group) == 0 else group
 
     def remote(src, dst, send, recv_sem, peer):
@@ -248,7 +249,7 @@
 
         each_near(lambda p: x_copy(j, p).start())
 
-    loop(0, held, send_chunk)
+    loop(0, min(ahead, held), send_chunk)
     own_lab.wait()
     for j in range(held):
         own_x_copy(j).wait()
@@ -287,6 +288,14 @@
         loop(0, half, fill_near)
         each_near(lambda p: x_arrival(j, p).wait_recv())
 
+        @pl.when(low)
+        def _():
+            each_far(lambda p: q_arrival(j, p).wait_recv())
+
+        @pl.when(j + ahead < held)
+        def _():
+            send_chunk(j + ahead)
+
         def keys_of(span):
             keys = recv[j, :span, :, size : 2 * size].reshape(span * tok, size)
             return jnp.concatenate([keys, cold[:span].reshape(span * tok, size)], axis=1)
@@ -301,7 +310,6 @@
                 hot[half + p] = jnp.where(label_match(half + p), 1.0, 0.0).astype(jnp.bfloat16)
 
             loop(0, half, fill_far)
-            each_far(lambda p: q_arrival(j, p).wait_recv())
             for first in range(0, half, wide):
                 query = jnp.concatenate([
                     qrecv[j, first : first + wide].reshape(wide * tok, size),

time: 93.4 us -> 89.6 us (0.959)
  Pallas kernels: 87.8 us -> 84 us
    pallas_call x1, Pallas kernels: 87.8 us -> 84 us  [by_head(): pl.pallas_call(functools.partial(exchange_kernel, nseq, held, group), out...]
where the time goes in v5:
time: 89.6 us; the launch traced here: 89.4 us
  Pallas kernels  84 us (94%)
  local copies, waits for them, and re-layouts  5.38 us (6%)
    pallas_call x1, Pallas kernels, by_head(): pl.pallas_call(functools.partial(exchange_kernel, nseq, held, group), out...  84 us
    unnamed x1, local copies, waits for them, and re-layouts  3.01 us

profile of v5, /device:TPU:31, one launch (start us, length us, event | category | flops | bytes accessed | tf_op | source)
XLA Modules:
  0.0 89.4 jit_solution(13965579483311341030)
XLA Ops:
  0.0 0.7 pad.4.lab_ref
  0.7 3.0 %copy.6 = bf16[128,32,384]{2,0,1:T(8,128)(2,1)S(1)} copy(bf16[128,32,384]{2,1,0:T(8,128)(2,1)} %param.2) | data formatting | bytes 6291456 | tf_op args[0]
  3.7 84.0 %exchange.1 = bf16[32,128,128]{2,1,0:T(8,128)(2,1)S(1)} custom-call(bf16[32,128,384]{2,1,0:T(8,128)(2,1)S(1)} %bitcast.7, s32[8,8,128]{2,1,0:T(8,128)S(1)} %pad.4.lab_ref), custom_call_target="tpu_custom_call" | custom-call | tf_op jit(solution)/shard_map/exchange/pallas_call | solution.py:418
  87.7 1.6 %copy.4 = bf16[128,32,128]{2,1,0:T(8,128)(2,1)} copy(bf16[128,32,128]{2,0,1:T(8,128)(2,1)S(1)} %bitcast.8) | data formatting | bytes 2097152 | tf_op jit(solution)/shard_map/transpose | solution.py:455

commit v6 on v5

--- a/solution.py
+++ b/solution.py
@@ -140,7 +140,7 @@
     size = width // 3
     scale = 1.0 / math.sqrt(size)
     rows = group * tok
-    ahead = 2
+    ahead = 1
     wide = 2 * group if half % (2 * group) == 0 else group
 
     def remote(src, dst, send, recv_sem, peer):

time: 89.6 us -> 98.8 us (1.10)
  Pallas kernels: 84 us -> 93.2 us
    pallas_call x1, Pallas kernels: 84 us -> 93.2 us  [by_head(): pl.pallas_call(functools.partial(exchange_kernel, nseq, held, group), out...]
where the time goes in v6:
time: 98.8 us; the launch traced here: 98.6 us
  Pallas kernels  93.2 us (94%)
  local copies, waits for them, and re-layouts  5.38 us (5%)
    pallas_call x1, Pallas kernels, by_head(): pl.pallas_call(functools.partial(exchange_kernel, nseq, held, group), out...  93.2 us
    unnamed x1, local copies, waits for them, and re-layouts  3.01 us

profile of v6, /device:TPU:31, one launch (start us, length us, event | category | flops | bytes accessed | tf_op | source)
XLA Modules:
  0.0 98.6 jit_solution(15804236208366352306)
XLA Ops:
  0.0 0.7 pad.4.lab_ref
  0.7 3.0 %copy.6 = bf16[128,32,384]{2,0,1:T(8,128)(2,1)S(1)} copy(bf16[128,32,384]{2,1,0:T(8,128)(2,1)} %param.2) | data formatting | bytes 6291456 | tf_op args[0]
  3.7 93.2 %exchange.1 = bf16[32,128,128]{2,1,0:T(8,128)(2,1)S(1)} custom-call(bf16[32,128,384]{2,1,0:T(8,128)(2,1)S(1)} %bitcast.7, s32[8,8,128]{2,1,0:T(8,128)S(1)} %pad.4.lab_ref), custom_call_target="tpu_custom_call" | custom-call | tf_op jit(solution)/shard_map/exchange/pallas_call | solution.py:418
  96.9 1.6 %copy.4 = bf16[128,32,128]{2,1,0:T(8,128)(2,1)} copy(bf16[128,32,128]{2,0,1:T(8,128)(2,1)S(1)} %bitcast.8) | data formatting | bytes 2097152 | tf_op jit(solution)/shard_map/transpose | solution.py:455

commit v7 on v5

--- a/solution.py
+++ b/solution.py
@@ -9,7 +9,6 @@
 from jax.sharding import PartitionSpec as P
 
 CLEN = 1024
-LABEL_ROWS = 8
 NEG = -1e36
 
 
@@ -249,7 +248,7 @@
 
         each_near(lambda p: x_copy(j, p).start())
 
-    loop(0, min(ahead, held), send_chunk)
+    send_chunk(0)
     own_lab.wait()
     for j in range(held):
         own_x_copy(j).wait()
@@ -291,6 +290,10 @@
         @pl.when(low)
         def _():
             each_far(lambda p: q_arrival(j, p).wait_recv())
+
+        @pl.when(j == 0)
+        def _():
+            loop(1, min(ahead, held), send_chunk)
 
         @pl.when(j + ahead < held)
         def _():
@@ -413,7 +416,6 @@
     held = heads // half
     group = 2 if half % 2 == 0 else 1
     lines = jnp.transpose(routes, (1, 0)).reshape(half, held, tok)
-    lines = jnp.pad(lines, ((0, 0), (0, LABEL_ROWS - held), (0, 0)))
     dma = pltpu.SemaphoreType.DMA
     out = pl.pallas_call(
         functools.partial(exchange_kernel, nseq, held, group),
@@ -423,7 +425,7 @@
         scratch_shapes=[
             pltpu.VMEM((held, half, tok, width), jnp.bfloat16),
             pltpu.VMEM((held, half, tok, size), jnp.bfloat16),
-            pltpu.VMEM((nseq, LABEL_ROWS, tok), jnp.int32),
+            pltpu.VMEM((nseq, held, tok), jnp.int32),
             pltpu.VMEM((held, nseq, tok, size), jnp.bfloat16),
             pltpu.VMEM((held, nseq, 8, tok), jnp.float32),
             pltpu.VMEM((2, heads, tok, size), jnp.bfloat16),
@@ -464,7 +466,7 @@
         half = nseq // 2
         clusters = nseq * qkv.shape[0] // CLEN
         fits = clusters <= qkv.shape[2] // 3
-        if fits and nseq % 2 == 0 and heads % half == 0 and heads // half <= LABEL_ROWS:
+        if fits and nseq % 2 == 0 and heads % half == 0:
             return by_head(qkv, routes)
         return routed(qkv, routes)
 

time: 89.6 us -> 96.1 us (1.073)
  Pallas kernels: 84 us -> 90.4 us
    pallas_call x1, Pallas kernels: 84 us -> 90.4 us  [by_head(): pl.pallas_call(functools.partial(exchange_kernel, nseq, held, group), out...]
    unnamed x1 -> x3, local copies, waits for them, and re-layouts: 3.01 us -> 3.03 us
where the time goes in v7:
time: 96.1 us; the launch traced here: 95.1 us
  Pallas kernels  90.4 us (94%)
  local copies, waits for them, and re-layouts  4.68 us (5%)
    pallas_call x1, Pallas kernels, by_head(): pl.pallas_call(functools.partial(exchange_kernel, nseq, held, group), out...  90.4 us
    unnamed x3, local copies, waits for them, and re-layouts  3.03 us

profile of v7, /device:TPU:31, one launch (start us, length us, event | category | flops | bytes accessed | tf_op | source)
XLA Modules:
  0.0 95.1 jit_solution(16471815128889752621)
XLA Ops:
  0.0 0.0 copy-start
  0.0 3.0 %copy.6 = bf16[128,32,384]{2,0,1:T(8,128)(2,1)S(1)} copy(bf16[128,32,384]{2,1,0:T(8,128)(2,1)} %param.2) | data formatting | bytes 6291456 | tf_op args[0]
  3.0 0.0 copy-done
  3.0 90.4 %exchange.1 = bf16[32,128,128]{2,1,0:T(8,128)(2,1)S(1)} custom-call(bf16[32,128,384]{2,1,0:T(8,128)(2,1)S(1)} %bitcast.7, s32[8,4,128]{2,1,0:T(4,128)S(1)} %bitcast.9), custom_call_target="tpu_custom_call" | custom-call | tf_op jit(solution)/shard_map/exchange/pallas_call | solution.py:420
  93.5 1.6 %copy.4 = bf16[128,32,128]{2,1,0:T(8,128)(2,1)} copy(bf16[128,32,128]{2,0,1:T(8,128)(2,1)S(1)} %bitcast.8) | data formatting | bytes 2097152 | tf_op jit(solution)/shard_map/transpose | solution.py:457
Async XLA Ops:
  0.0 3.0 %copy-start = (s32[128,32]{0,1:T(8,128)S(1)}, s32[128,32]{0,1:T(8,128)}, u32[]{:S(2)}) copy-start(s32[128,32]{0,1:T(8,128)} %param.3) | copy-start | bytes 49156

commit v8 on v7

--- a/solution.py
+++ b/solution.py
@@ -124,8 +124,8 @@
 
 
 def exchange_kernel(
-    nseq, held, group, x_ref, lab_ref, out_ref, recv, qrecv, labs, obuf, sbuf, part, stats, merged, hot, cold,
-    x_send, x_recv, q_send, q_recv, l_send, l_recv, o_send, o_recv, s_send, s_recv,
+    nseq, held, group, x_ref, lab_ref, out_ref, recv, qrecv, kvrecv, labs, obuf, sbuf, part, stats, merged, hot, cold,
+    x_send, x_recv, q_send, q_recv, kv_send, kv_recv, l_send, l_recv, o_send, o_recv, s_send, s_recv,
     own_x, own_l, own_o, own_s, m_sem,
 ):
     me = lax.axis_index("seq")
@@ -140,6 +140,7 @@
     scale = 1.0 / math.sqrt(size)
     rows = group * tok
     ahead = 2
+    direct = held - 1
     wide = 2 * group if half % (2 * group) == 0 else group
 
     def remote(src, dst, send, recv_sem, peer):
@@ -170,13 +171,21 @@
     def l_arrival(peer):
         return remote(lab_ref.at[0], labs.at[peer], l_send.at[peer], l_recv.at[peer], peer)
 
-    def o_copy_low(j, p):
-        return remote(obuf.at[j, p], out_ref.at[mine * held + j],
-                      o_send.at[j, p], o_recv.at[0, j, mine], p)
-
-    def o_arrival_low(j, p):
+    def kv_copy(p):
+        return remote(x_ref.at[p * held + direct, :, pl.ds(size, 2 * size)], kvrecv.at[mine],
+                      kv_send.at[p], kv_recv.at[mine], half + p)
+
+    def kv_arrival(p):
+        return remote(x_ref.at[0, :, pl.ds(size, 2 * size)], kvrecv.at[p],
+                      kv_send.at[p], kv_recv.at[p], p)
+
+    def f_copy(j, p):
+        return remote(obuf.at[j, base + p], out_ref.at[mine * held + j],
+                      o_send.at[j, base + p], o_recv.at[side, j, mine], base + p)
+
+    def f_arrival(j, p):
         return remote(obuf.at[j, 0], out_ref.at[p * held + j],
-                      o_send.at[j, p], o_recv.at[0, j, p], p)
+                      o_send.at[j, base + p], o_recv.at[side, j, p], base + p)
 
     def o_copy_up(j, peer):
         return remote(obuf.at[j, peer], part.at[side, mine * held + j],
@@ -197,7 +206,7 @@
     def own_x_copy(j):
         return pltpu.make_async_copy(x_ref.at[mine * held + j], recv.at[j, mine], own_x.at[j])
 
-    def own_o_low(j):
+    def own_f(j):
         return pltpu.make_async_copy(obuf.at[j, me], out_ref.at[mine * held + j], own_o.at[j])
 
     def own_o_up(j):
@@ -235,28 +244,25 @@
         barrier, inc=1, device_id={"seq": peer}, device_id_type=pl.DeviceIdType.MESH))
     pl.semaphore_wait(barrier, nseq - 1)
 
-    each_near(lambda p: l_copy(base + p).start())
-
-    @pl.when(up)
-    def _():
-        each_far(lambda p: l_copy(p).start())
+    each_peer(lambda peer: l_copy(peer).start())
 
     def send_chunk(j):
-        @pl.when(up)
+        @pl.when(up & (j < direct))
         def _():
             each_far(lambda p: q_copy(j, p).start())
 
         each_near(lambda p: x_copy(j, p).start())
 
-    send_chunk(0)
+    loop(0, min(ahead, held), send_chunk)
+
+    @pl.when(low)
+    def _():
+        each_far(lambda p: kv_copy(p).start())
+
     own_lab.wait()
     for j in range(held):
         own_x_copy(j).wait()
-    each_near(lambda p: l_arrival(base + p).wait_recv())
-
-    @pl.when(low)
-    def _():
-        each_far(lambda p: l_arrival(half + p).wait_recv())
+    each_peer(lambda peer: l_arrival(peer).wait_recv())
 
     eye = lax.broadcasted_iota(jnp.int32, (tok, tok), 0) == lax.broadcasted_iota(
         jnp.int32, (tok, tok), 1)
@@ -274,68 +280,81 @@
             sbuf[j, first + g, 0:1, :] = to_row(peak[part_rows])
             sbuf[j, first + g, 1:2, :] = to_row(total[part_rows])
 
-    def chunk(j):
-        def label_match(source):
-            col = to_col(labs[source, pl.ds(j, 1), :])
-            return lax.broadcasted_iota(jnp.int32, (tok, size), 1) == col
-
+    def label_match(j, source):
+        col = to_col(labs[source, pl.ds(j, 1), :])
+        return lax.broadcasted_iota(jnp.int32, (tok, size), 1) == col
+
+    def fill_hot(j, source):
+        hot[source] = jnp.where(label_match(j, source), 1.0, 0.0).astype(jnp.bfloat16)
+
+    def fill_cold(j, source):
+        cold[source] = jnp.where(label_match(j, source), 0.0, NEG).astype(jnp.bfloat16)
+
+    def arrive(j):
         def fill_near(p):
-            match = label_match(base + p)
-            hot[base + p] = jnp.where(match, 1.0, 0.0).astype(jnp.bfloat16)
-            cold[p] = jnp.where(match, 0.0, NEG).astype(jnp.bfloat16)
+            fill_hot(j, base + p)
+            fill_cold(j, base + p)
 
         loop(0, half, fill_near)
         each_near(lambda p: x_arrival(j, p).wait_recv())
+
+    def with_ones(values):
+        return jnp.concatenate([values, jnp.ones(values.shape, jnp.bfloat16)], axis=1)
+
+    def keys_of(j, span):
+        keys = recv[j, :span, :, size : 2 * size].reshape(span * tok, size)
+        return jnp.concatenate(
+            [keys, cold[pl.ds(base, span)].reshape(span * tok, size)], axis=1)
+
+    def values_of(j, span):
+        return with_ones(recv[j, :span, :, 2 * size :].reshape(span * tok, size))
+
+    def causal_blocks(j, keys_low=None, values_low=None):
+        for first in range(0, half, group):
+            query = jnp.concatenate([
+                recv[j, first : first + group, :, :size].reshape(rows, size),
+                hot[pl.ds(base + first, group)].reshape(rows, size)], axis=1)
+            keys, values = keys_of(j, first + group), values_of(j, first + group)
+            if keys_low is not None:
+                keys = jnp.concatenate([keys_low(), keys], axis=0)
+                values = jnp.concatenate([values_low(), values], axis=0)
+            result, peak, total = partial_softmax(query, keys, values, scale, True)
+            keep(j, base + first, group, result, peak, total)
+
+    def send_final(j):
+        each_near(lambda p: f_copy(j, p).start())
+        own_f(j).start()
+
+    def chunk(j):
+        arrive(j)
 
         @pl.when(low)
         def _():
             each_far(lambda p: q_arrival(j, p).wait_recv())
 
-        @pl.when(j == 0)
-        def _():
-            loop(1, min(ahead, held), send_chunk)
-
         @pl.when(j + ahead < held)
         def _():
             send_chunk(j + ahead)
 
-        def keys_of(span):
-            keys = recv[j, :span, :, size : 2 * size].reshape(span * tok, size)
-            return jnp.concatenate([keys, cold[:span].reshape(span * tok, size)], axis=1)
-
-        def values_of(span):
-            values = recv[j, :span, :, 2 * size :].reshape(span * tok, size)
-            return jnp.concatenate([values, jnp.ones((span * tok, size), jnp.bfloat16)], axis=1)
-
         @pl.when(low)
         def _():
-            def fill_far(p):
-                hot[half + p] = jnp.where(label_match(half + p), 1.0, 0.0).astype(jnp.bfloat16)
-
-            loop(0, half, fill_far)
+            loop(0, half, lambda p: fill_hot(j, half + p))
             for first in range(0, half, wide):
                 query = jnp.concatenate([
                     qrecv[j, first : first + wide].reshape(wide * tok, size),
                     hot[half + first : half + first + wide].reshape(wide * tok, size)], axis=1)
                 result, peak, total = partial_softmax(
-                    query, keys_of(half), values_of(half), scale, False)
+                    query, keys_of(j, half), values_of(j, half), scale, False)
                 keep(j, half + first, wide, result, peak, total)
                 for g in range(wide):
                     o_copy_up(j, half + first + g).start()
                     s_copy(j, half + first + g).start()
 
-        for first in range(0, half, group):
-            query = jnp.concatenate([
-                recv[j, first : first + group, :, :size].reshape(rows, size),
-                hot[pl.ds(base + first, group)].reshape(rows, size)], axis=1)
-            result, peak, total = partial_softmax(
-                query, keys_of(first + group), values_of(first + group), scale, True)
-            keep(j, base + first, group, result, peak, total)
+        causal_blocks(j)
 
         @pl.when(low)
         def _():
-            each_near(lambda p: o_copy_low(j, p).start())
-            own_o_low(j).start()
+            send_final(j)
 
         @pl.when(up)
         def _():
@@ -347,33 +366,59 @@
             own_o_up(j).start()
             own_s_up(j).start()
 
-    loop(0, held, chunk)
-
-    each_near(lambda p: l_copy(base + p).wait_send())
-    loop(0, held, lambda j: each_near(lambda p: x_copy(j, p).wait_send()))
+    loop(0, direct, chunk)
+    arrive(direct)
 
     @pl.when(low)
     def _():
+        causal_blocks(direct)
+
+    @pl.when(up)
+    def _():
+        loop(0, half, lambda p: fill_cold(direct, p))
+        each_far(lambda p: kv_arrival(p).wait_recv())
+
+        def keys_low():
+            keys = kvrecv[:, :, :size].reshape(half * tok, size)
+            return jnp.concatenate([keys, cold[:half].reshape(half * tok, size)], axis=1)
+
+        def values_low():
+            return with_ones(kvrecv[:, :, size:].reshape(half * tok, size))
+
+        causal_blocks(direct, keys_low, values_low)
+
+    send_final(direct)
+
+    each_peer(lambda peer: l_copy(peer).wait_send())
+    loop(0, held, lambda j: each_near(lambda p: x_copy(j, p).wait_send()))
+
+    def finish_final(j):
+        own_f(j).wait()
+
+        def near(p):
+            f_copy(j, p).wait_send()
+            f_arrival(j, p).wait_recv()
+
+        each_near(near)
+
+    @pl.when(low)
+    def _():
+        each_far(lambda p: kv_copy(p).wait_send())
+
         def finish(j):
-            own_o_low(j).wait()
-
-            def near(p):
-                o_copy_low(j, p).wait_send()
-                o_arrival_low(j, p).wait_recv()
+            finish_final(j)
 
             def far(p):
                 o_copy_up(j, half + p).wait_send()
                 s_copy(j, half + p).wait_send()
 
-            each_near(near)
             each_far(far)
 
-        loop(0, held, finish)
+        loop(0, direct, finish)
 
     @pl.when(up)
     def _():
-        each_far(lambda p: l_copy(p).wait_send())
-        loop(0, held, lambda j: each_far(lambda p: q_copy(j, p).wait_send()))
+        loop(0, direct, lambda j: each_far(lambda p: q_copy(j, p).wait_send()))
 
         def finish(j):
             own_o_up(j).wait()
@@ -404,8 +449,10 @@
 
             loop(0, half, merge)
 
-        loop(0, held, finish)
-        loop(0, half * held, lambda head: result_copy(head).wait())
+        loop(0, direct, finish)
+        loop(0, direct, lambda j: each_far(lambda p: result_copy(p * held + j).wait()))
+
+    finish_final(direct)
 
 
 def by_head(qkv, routes):
@@ -425,6 +472,7 @@
         scratch_shapes=[
             pltpu.VMEM((held, half, tok, width), jnp.bfloat16),
             pltpu.VMEM((held, half, tok, size), jnp.bfloat16),
+            pltpu.VMEM((half, tok, 2 * size), jnp.bfloat16),
             pltpu.VMEM((nseq, held, tok), jnp.int32),
             pltpu.VMEM((held, nseq, tok, size), jnp.bfloat16),
             pltpu.VMEM((held, nseq, 8, tok), jnp.float32),
@@ -432,11 +480,13 @@
             pltpu.VMEM((2, half, held, 8, tok), jnp.float32),
             pltpu.VMEM((heads, tok, size), jnp.bfloat16),
             pltpu.VMEM((nseq, tok, size), jnp.bfloat16),
-            pltpu.VMEM((half, tok, size), jnp.bfloat16),
+            pltpu.VMEM((nseq, tok, size), jnp.bfloat16),
             dma((held, half)),
             dma((held, half)),
             dma((held, half)),
             dma((held, half)),
+            dma((half,)),
+            dma((half,)),
             dma((nseq,)),
             dma((nseq,)),
             dma((held, nseq)),

time: 96.1 us -> 93 us (0.968)
  the two profiles are of different devices: /device:TPU:31 before, /device:TPU:0 now
where the time goes in v8:
time: 93 us; the launch traced here: 92.9 us
  Pallas kernels  88.2 us (95%)
  local copies, waits for them, and re-layouts  4.68 us (5%)
    pallas_call x1, Pallas kernels, by_head(): pl.pallas_call(functools.partial(exchange_kernel, nseq, held, group), out...  88.2 us
    unnamed x3, local copies, waits for them, and re-layouts  3.03 us

profile of v8, /device:TPU:0, one launch (start us, length us, event | category | flops | bytes accessed | tf_op | source)
XLA Modules:
  0.0 92.9 jit_solution(1282485755063155159)
XLA Ops:
  0.0 0.0 copy-start
  0.0 3.0 %copy.6 = bf16[128,32,384]{2,0,1:T(8,128)(2,1)S(1)} copy(bf16[128,32,384]{2,1,0:T(8,128)(2,1)} %param.2) | data formatting | bytes 6291456 | tf_op args[0]
  3.0 0.0 copy-done
  3.0 88.2 %exchange.1 = bf16[32,128,128]{2,1,0:T(8,128)(2,1)S(1)} custom-call(bf16[32,128,384]{2,1,0:T(8,128)(2,1)S(1)} %bitcast.7, s32[8,4,128]{2,1,0:T(4,128)S(1)} %bitcast.9), custom_call_target="tpu_custom_call" | custom-call | tf_op jit(solution)/shard_map/exchange/pallas_call | solution.py:467
  91.2 1.6 %copy.4 = bf16[128,32,128]{2,1,0:T(8,128)(2,1)} copy(bf16[128,32,128]{2,0,1:T(8,128)(2,1)S(1)} %bitcast.8) | data formatting | bytes 2097152 | tf_op jit(solution)/shard_map/transpose | solution.py:507
Async XLA Ops:
  0.0 3.0 %copy-start = (s32[128,32]{0,1:T(8,128)S(1)}, s32[128,32]{0,1:T(8,128)}, u32[]{:S(2)}) copy-start(s32[128,32]{0,1:T(8,128)} %param.3) | copy-start | bytes 49156

commit v9 on v7

--- a/solution.py
+++ b/solution.py
@@ -246,9 +246,10 @@
         def _():
             each_far(lambda p: q_copy(j, p).start())
 
-        each_near(lambda p: x_copy(j, p).start())
-
-    send_chunk(0)
+        for k in sorted(range(1, half), key=lambda k: abs(2 * k - half)):
+            x_copy(j, lax.rem(mine + k, half)).start()
+
+    loop(0, min(ahead, held), send_chunk)
     own_lab.wait()
     for j in range(held):
         own_x_copy(j).wait()
@@ -290,10 +291,6 @@
         @pl.when(low)
         def _():
             each_far(lambda p: q_arrival(j, p).wait_recv())
-
-        @pl.when(j == 0)
-        def _():
-            loop(1, min(ahead, held), send_chunk)
 
         @pl.when(j + ahead < held)
         def _():

time: 96.1 us -> 88.7 us (0.923)
  Pallas kernels: 90.4 us -> 83.8 us
    pallas_call x1, Pallas kernels: 90.4 us -> 83.8 us  [by_head(): pl.pallas_call(functools.partial(exchange_kernel, nseq, held, group), out...]
where the time goes in v9:
time: 88.7 us; the launch traced here: 88.5 us
  Pallas kernels  83.8 us (94%)
  local copies, waits for them, and re-layouts  4.68 us (5%)
    pallas_call x1, Pallas kernels, by_head(): pl.pallas_call(functools.partial(exchange_kernel, nseq, held, group), out...  83.8 us
    unnamed x3, local copies, waits for them, and re-layouts  3.03 us

profile of v9, /device:TPU:31, one launch (start us, length us, event | category | flops | bytes accessed | tf_op | source)
XLA Modules:
  0.0 88.5 jit_solution(17738831826496058633)
XLA Ops:
  0.0 0.0 copy-start
  0.0 3.0 %copy.6 = bf16[128,32,384]{2,0,1:T(8,128)(2,1)S(1)} copy(bf16[128,32,384]{2,1,0:T(8,128)(2,1)} %param.2) | data formatting | bytes 6291456 | tf_op args[0]
  3.0 0.0 copy-done
  3.0 83.8 %exchange.1 = bf16[32,128,128]{2,1,0:T(8,128)(2,1)S(1)} custom-call(bf16[32,128,384]{2,1,0:T(8,128)(2,1)S(1)} %bitcast.7, s32[8,4,128]{2,1,0:T(4,128)S(1)} %bitcast.9), custom_call_target="tpu_custom_call" | custom-call | tf_op jit(solution)/shard_map/exchange/pallas_call | solution.py:417
  86.9 1.6 %copy.4 = bf16[128,32,128]{2,1,0:T(8,128)(2,1)} copy(bf16[128,32,128]{2,0,1:T(8,128)(2,1)S(1)} %bitcast.8) | data formatting | bytes 2097152 | tf_op jit(solution)/shard_map/transpose | solution.py:454
Async XLA Ops:
  0.0 3.0 %copy-start = (s32[128,32]{0,1:T(8,128)S(1)}, s32[128,32]{0,1:T(8,128)}, u32[]{:S(2)}) copy-start(s32[128,32]{0,1:T(8,128)} %param.3) | copy-start | bytes 49156
